TPU v7x, 512 devices: a whole 4x8x8 slice. The times are simulated.
512 devices in a mesh: tm: 8 (over z_hi, core), particle: 8 (over y), cell: 8 (over x, z_lo).
Axes of the slice: x: 4, y: 8, z: 8 (z_hi: 4, z_lo: 2; z = z_hi * 2 + z_lo), core: 2. Of those that a mesh axis runs over, the one named last changes fastest.
Arguments:
- particles: float32 [8, 30, 8192], P('tm', None, 'particle'), may hold values from -50 to 50
- cell_points: float32 [8, 30, 8192], P('tm', None, 'cell'), may hold values from -50 to 50
- cell_counts: int32 [8], replicated, may hold values from 1365 to 8192, as said below
- brownian: float32 [8, 30, 8192], P('tm', None, ('particle', 'cell')), may hold values from -6 to 6
Outputs:
- descent_direction: float32 [8, 30, 8192], P('tm', None, ('particle', 'cell'))
- updated_particles: float32 [8, 30, 8192], P('tm', None, ('particle', 'cell'))
Inputs may be any that keep to these rules, and one draw needn't show every extreme that they name: `cell_counts`: some time has all 8192 cells observed.
All inputs are finite; a program needn't handle non-finite values.
Results may differ from a plain program's by a relative error of at most 0.0003.
Values sent between devices are 32-bit elements; how exact they have to be, the bound alone decides.
A program may use at most 64 MiB of HBM per device.

v0:
```python
import math
import jax
import jax.numpy as jnp
from jax import lax
from jax.sharding import PartitionSpec as P

DATA_VAR = 2.0
BRIDGE_VAR = 1.5
LANGEVIN_STRIDE = 0.05
NOISE_LEVEL = 1.0
lowest_score = -1e30


def joined(x, axis, combine):
    everything = jax.tree.map(lambda part: lax.all_gather(part, axis), x)
    first = jax.tree.map(lambda part: part[0], everything)

    def turn(k, so_far):
        return combine(so_far, jax.tree.map(lambda part: part[k], everything))

    return lax.fori_loop(1, lax.axis_size(axis), turn, first)


def passed_along(x, axis, by):
    count = lax.axis_size(axis)
    pairs = [(i, i + by) for i in range(count) if 0 <= i + by < count]
    return lax.ppermute(x, axis, pairs)


def fresh_state(feature_count, row_count):
    return (
        jnp.full((row_count,), lowest_score, jnp.float32),
        jnp.zeros((row_count,), jnp.float32),
        jnp.zeros((feature_count, row_count), jnp.float32),
    )


def fold_targets(running, queries, query_sq, targets, usable, spread):
    highest_seen, summed, weighted = running
    cross_terms = lax.dot_general(
        queries,
        targets,
        (((0,), (0,)), ((), ())),
        precision=lax.Precision.HIGHEST,
        preferred_element_type=jnp.float32,
    )
    scores = (2.0 * cross_terms - query_sq[:, None] - jnp.sum(targets * targets, 0)[None, :]) / (
        2.0 * spread
    )
    scores = jnp.where(usable[None, :], scores, lowest_score)
    new_high = jnp.maximum(highest_seen, jnp.max(scores, 1))
    factor = jnp.exp(highest_seen - new_high)
    expo_terms = jnp.where(usable[None, :], jnp.exp(scores - new_high[:, None]), 0.0)
    summed = summed * factor + jnp.sum(expo_terms, 1)
    weighted = weighted * factor[None, :] + lax.dot_general(
        targets,
        expo_terms,
        (((1,), (1,)), ((), ())),
        precision=lax.Precision.HIGHEST,
        preferred_element_type=jnp.float32,
    )
    return (new_high, summed, weighted)


def sweep(running, queries, query_sq, targets, spread, first_key, key_limit):
    key_span = math.gcd(targets.shape[1], 512)
    key_rounds = targets.shape[1] // key_span

    def visit(turn_index, carried):
        offset = turn_index * key_span
        key_block = lax.dynamic_slice_in_dim(targets, offset, key_span, 1)
        usable = first_key + offset + jnp.arange(key_span, dtype=jnp.int32) < key_limit
        return fold_targets(carried, queries, query_sq, key_block, usable, spread)

    return lax.fori_loop(0, key_rounds, visit, running)


def combine_parts(earlier_part, later_part):
    new_high = jnp.maximum(earlier_part[0], later_part[0])
    scale_first = jnp.exp(earlier_part[0] - new_high)
    scale_second = jnp.exp(later_part[0] - new_high)
    summed = earlier_part[1] * scale_first + later_part[1] * scale_second
    weighted = earlier_part[2] * scale_first[None, :] + later_part[2] * scale_second[None, :]
    return (new_high, summed, weighted)


def shards(particles, cell_points, cell_counts, brownian):
    own_block = particles[0]
    own_cells = cell_points[0]
    feature_count = own_block.shape[0]
    block_rows = own_block.shape[1]
    share_width = block_rows // lax.axis_size("cell")
    cell_index = lax.axis_index("cell")
    time_index = lax.axis_index("tm")
    share_start = cell_index * share_width
    local_portion = lax.dynamic_slice_in_dim(own_block, share_start, share_width, 1)
    cell_limit = jnp.sum(
        jnp.where(jnp.arange(cell_counts.shape[0], dtype=jnp.int32) == time_index, cell_counts, 0)
    )
    first_cell = cell_index * own_cells.shape[1]
    block_sq = jnp.sum(own_block * own_block, 0)
    starting = fresh_state(feature_count, block_rows)
    fit_state = sweep(starting, own_block, block_sq, own_cells, DATA_VAR, first_cell, cell_limit)
    fit_high, fit_sum, fit_weighted = joined(
        (fit_state[0], fit_state[1], fit_state[2]), "cell", combine_parts
    )
    share_sum = lax.dynamic_slice_in_dim(fit_sum, share_start, share_width, 0)
    share_weighted = lax.dynamic_slice_in_dim(fit_weighted, share_start, share_width, 1)
    fit_mean = share_weighted / share_sum[None, :]
    share_sq = jnp.sum(local_portion * local_portion, 0)
    share_start_state = fresh_state(feature_count, share_width)
    earlier = passed_along(local_portion, "tm", 1)
    following = passed_along(local_portion, "tm", -1)
    prior_piece = lax.all_gather(earlier, ("particle", "cell"), axis=1, tiled=True)
    later_piece = lax.all_gather(following, ("particle", "cell"), axis=1, tiled=True)
    prior_state = sweep(
        share_start_state, local_portion, share_sq, prior_piece, BRIDGE_VAR, 0, prior_piece.shape[1]
    )
    later_state = sweep(
        share_start_state, local_portion, share_sq, later_piece, BRIDGE_VAR, 0, later_piece.shape[1]
    )
    prior_mean = prior_state[2] / prior_state[1][None, :]
    later_mean = later_state[2] / later_state[1][None, :]
    has_prior = (time_index > 0).astype(jnp.float32)
    has_later = (time_index < lax.axis_size("tm") - 1).astype(jnp.float32)
    gradient = (local_portion - fit_mean) / DATA_VAR
    gradient = gradient + has_prior * (local_portion - prior_mean) / BRIDGE_VAR
    gradient = gradient + has_later * (local_portion - later_mean) / BRIDGE_VAR
    descent_direction = -gradient
    updated_particles = (
        local_portion
        + LANGEVIN_STRIDE * descent_direction
        + math.sqrt(2.0 * LANGEVIN_STRIDE * NOISE_LEVEL) * brownian[0]
    )
    return (descent_direction[None], updated_particles[None])


def solution(mesh):
    in_specs = (
        P("tm", None, "particle"),
        P("tm", None, "cell"),
        P(),
        P("tm", None, ("particle", "cell")),
    )
    out_specs = (P("tm", None, ("particle", "cell")), P("tm", None, ("particle", "cell")))
    return jax.shard_map(shards, mesh=mesh, in_specs=in_specs, out_specs=out_specs, check_vma=False)
```

profile of v0, /device:TPU:128, one launch (start us, length us, event | category | flops | bytes accessed | tf_op | source)
XLA Modules:
  0.0 495.2 jit_solution(1083620822759951898)
XLA Ops:
  2.0 1.9 collective-permute-start
  3.9 4.5 collective-permute-start.1
  12.5 9.7 %while.74 = (s32[]{:T(128)}, f32[1024]{0:T(1024)S(1)}, f32[1024]{0:T(1024)S(1)}, f32[30,1024]{1,0:T(8,128)S(1)}, s32[]{:T(128)}, /*index=5*/s32[]{:T(128)}, f32[...) while((s32[]{:T(128)}, f32[1024]{0:T(1024)S(1)}, ...), condition=%wide.region_6.7_spmd.clone, body=%wide.region_2.6_spmd.clone.sunk | while | flops 383383040 | bytes 6944983 | solution.py:75
  13.1 2.2 fusion.74
  15.8 1.6 fusion.77
  18.0 2.2 fusion.74
  20.6 1.6 fusion.77
  22.2 28.5 %all-gather = f32[8192]{0:T(1024)S(1)} all-gather(f32[1024]{0:T(1024)S(1)} %get-tuple-element.585), channel_id=2, replica_groups=mesh['tm'=8,'particle'=8,'cell'=8] {'cell'}, dimensions={0}, use_global_device_ids=true | all-gather | bytes 36864 | tf_op jit(solution)/shard_map/all_gather | solution.py:15
  50.8 28.1 %all-gather.1 = f32[8192]{0:T(1024)S(1)} all-gather(f32[1024]{0:T(1024)S(1)} %get-tuple-element.586), channel_id=3, replica_groups=mesh['tm'=8,'particle'=8,'cell'=8] {'cell'}, dimensions={0}, use_global_device_ids=true | all-gather | bytes 36864 | tf_op jit(solution)/shard_map/all_gather | solution.py:15
  78.9 32.9 %all-gather.3 = f32[8,30,1024]{2,1,0:T(8,128)S(1)} all-gather(f32[1,30,1024]{2,1,0:T(8,128)S(1)} %bitcast.44), channel_id=4, replica_groups=mesh['tm'=8,'particle'=8,'cell'=8] {'cell'}, dimensions={0}, use_global_device_ids=true | all-gather | bytes 1105920 | tf_op jit(solution)/shard_map/all_gather | solution.py:15
  112.8 161.8 %all_gather.30 = f32[30,8192]{1,0:T(8,128)S(1)} all-gather(f32[30,128]{1,0:T(8,128)S(1)} %collective-permute-done), channel_id=1, replica_groups=mesh['tm'=8,'particle'=8,'cell'=8] {'particle','cell'}, dimensions={1}, use_global_device_ids=true | all-gather | bytes 998400 | tf_op jit(solution)/shard_map/all_gather | solution.py:114
  274.5 31.9 %while.75 = (s32[]{:T(128)}, f32[128]{0:T(128)S(1)}, f32[128]{0:T(128)S(1)}, f32[30,128]{1,0:T(8,128)S(1)}, f32[30,8192]{1,0:T(8,128)S(1)}, /*index=5*/f32[30,12...) while((s32[]{:T(128)}, f32[128]{0:T(128)S(1)}, ...), condition=%wide.region_14.15_spmd.clone, body=%wide.region_10.14_spmd.clone.sunk | while | flops 47950212 | bytes 1041079 | solution.py:75
  274.6 1.4 fusion.80
  276.6 1.4 fusion.80
  278.6 1.4 fusion.80
  280.6 1.4 fusion.80
  282.6 1.4 fusion.80
  286.5 1.4 fusion.80
  288.5 1.4 fusion.80
  290.5 1.4 fusion.80
  292.5 1.4 fusion.80
  294.5 1.4 fusion.80
  306.4 155.6 %all_gather.31 = f32[30,8192]{1,0:T(8,128)S(1)} all-gather(f32[30,128]{1,0:T(8,128)S(1)} %collective-permute-done.1), channel_id=1, replica_groups=mesh['tm'=8,'particle'=8,'cell'=8] {'particle','cell'}, dimensions={1}, use_global_device_ids=true | all-gather | bytes 998400 | tf_op jit(solution)/shard_map/all_gather | solution.py:115
  462.1 31.9 %while.76 = (s32[]{:T(128)}, f32[128]{0:T(128)S(1)}, f32[128]{0:T(128)S(1)}, f32[30,128]{1,0:T(8,128)S(1)}, f32[30,8192]{1,0:T(8,128)S(1)}, /*index=5*/f32[30,12...) while((s32[]{:T(128)}, f32[128]{0:T(128)S(1)}, ...), condition=%wide.region_19.20_spmd.clone, body=%wide.region_15.19_spmd.clone.sunk | while | flops 47950212 | bytes 1041079 | solution.py:75
  (309 shorter events, 58.4 us)
Async XLA Ops:
  2.0 110.8 %collective-permute-start = (f32[30,128]{1,0:T(8,128)}, f32[30,128]{1,0:T(8,128)S(1)}, u32[]{:S(2)}, u32[]{:S(2)}) collective-permute-start(f32[30,128]{1,0:T(8,128)} %bitcast.31), channel_id=1, source_target_pairs={{0,64},{64,128},{128,192},{192,256},{256,320},{320,384},{384,448},... | collective-permute-start | bytes 46088 | tf_op jit(solution)/shard_map/ppermute | solution.py:27
  3.9 302.6 %collective-permute-start.1 = (f32[30,128]{1,0:T(8,128)}, f32[30,128]{1,0:T(8,128)S(1)}, u32[]{:S(2)}, u32[]{:S(2)}) collective-permute-start(f32[30,128]{1,0:T(8,128)} %bitcast.31), channel_id=1, source_target_pairs={{64,0},{128,64},{192,128},{256,192},{320,256},{384,320},{448,384},... | collective-permute-start | bytes 46088 | tf_op jit(solution)/shard_map/ppermute | solution.py:27
  462.1 31.9 %copy-start = (f32[1,30,128]{2,0,1:T(1,128)S(1)}, f32[1,30,128]{2,0,1:T(1,128)}, u32[]{:S(2)}) copy-start(f32[1,30,128]{2,0,1:T(1,128)} %param.15) | copy-start | bytes 46084
where the time goes:
time: 498 us; the launch traced here: 495 us
  blocking collectives  407 us (82%)
  matrix products  62.8 us (13%)
  other arithmetic  11.4 us (2%)
  starting transfers between devices  6.45 us (1%)
    all_gather x1, blocking collectives, shards(): lax.all_gather(earlier, ('particle', 'cell'), axis=1, tiled=True)  162 us
    all_gather x1, blocking collectives, shards(): lax.all_gather(following, ('particle', 'cell'), axis=1, tiled=True)  156 us
    all_gather x3, blocking collectives, joined(): everything = jax.tree.map(lambda part: lax.all_gather(part, axis), x)  89.5 us
    dot_general x34, matrix products, fold_targets(): lax.dot_general(queries, targets, (((0,), (0,)), ((), ())), precision=lax...  48.1 us
    dot_general x34, matrix products, fold_targets(): lax.dot_general(targets, expo_terms, (((1,), (1,)), ((), ())), precision=...  14.7 us
  transfers between devices with their start and end apart: 2, of which 0 were waited for; matrix products, arithmetic and copies ran while one was open for 9% of the time, Pallas kernels for 0%

commit v1 on v0

--- a/solution.py
+++ b/solution.py
@@ -111,7 +111,12 @@
     share_start_state = fresh_state(feature_count, share_width)
     earlier = passed_along(local_portion, "tm", 1)
     following = passed_along(local_portion, "tm", -1)
-    prior_piece = lax.all_gather(earlier, ("particle", "cell"), axis=1, tiled=True)
+    prior_piece = jnp.concatenate(
+        lax.all_to_all(
+            jnp.stack([earlier] * lax.axis_size(("particle", "cell"))), ("particle", "cell"), 0, 0
+        ),
+        axis=1,
+    )
     later_piece = lax.all_gather(following, ("particle", "cell"), axis=1, tiled=True)
     prior_state = sweep(
         share_start_state, local_portion, share_sq, prior_piece, BRIDGE_VAR, 0, prior_piece.shape[1]

time: 498 us -> 337 us (0.68)
  the two profiles are of different devices: /device:TPU:128 before, /device:TPU:160 now
where the time goes in v1:
time: 337 us
  blocking collectives  256 us (76%)
  matrix products  39.8 us (12%)
  starting transfers between devices  19.1 us (6%)
  other arithmetic  11.7 us (3%)
  local copies, waits for them, and re-layouts  6.53 us (2%)
    all_gather x1, blocking collectives, shards(): lax.all_gather(following, ('particle', 'cell'), axis=1, tiled=True)  167 us
    all_gather x3, blocking collectives, joined(): everything = jax.tree.map(lambda part: lax.all_gather(part, axis), x)  89.8 us
    dot_general x34, matrix products, fold_targets(): lax.dot_general(queries, targets, (((0,), (0,)), ((), ())), precision=lax...  25.1 us
    dot_general x34, matrix products, fold_targets(): lax.dot_general(targets, expo_terms, (((1,), (1,)), ((), ())), precision=...  14.7 us
    all_to_all x1, starting transfers between devices, shards(): lax.all_to_all(jnp.stack([earlier] * lax.axis_size(('particle', 'cell')))...  12.7 us
  transfers between devices with their start and end apart: 3, of which 0 were waited for; matrix products, arithmetic and copies ran while one was open for 10% of the time, Pallas kernels for 0%

profile of v1, /device:TPU:160, one launch (start us, length us, event | category | flops | bytes accessed | tf_op | source)
XLA Modules:
  0.0 336.6 jit_solution(10002768272859447811)
XLA Ops:
  0.6 0.7 constant_dynamic-slice_fusion.2
  1.4 1.9 collective-permute-start
  3.3 4.5 %collective-permute-start.1 = (f32[30,128]{1,0:T(8,128)S(1)}, f32[30,128]{1,0:T(8,128)S(1)}, u32[]{:S(2)}, u32[]{:S(2)}) collective-permute-start(f32[30,128]{1,0:T(8,128)S(1)} %bitcast.57), channel_id=1, source_target_pairs={{64,0},{128,64},{192,128},{256,192},{320,256},{384,320},{448,384},... | collective-permute-start | bytes 46088 | tf_op jit(solution)/shard_map/ppermute | solution.py:27
  7.8 0.9 copy.29
  8.8 0.9 multiply_reduce_fusion.3
  9.7 0.9 copy.30
  10.7 1.4 fusion.45
  12.0 9.9 %while.74 = (s32[]{:T(128)}, f32[1024]{0:T(1024)S(1)}, f32[1024]{0:T(1024)S(1)}, f32[30,1024]{1,0:T(8,128)S(1)}, s32[]{:T(128)}, /*index=5*/s32[]{:T(128)}, f32[...) while((s32[]{:T(128)}, f32[1024]{0:T(1024)S(1)}, ...), condition=%wide.region_6.7_spmd.clone, body=%wide.region_2.6_spmd.clone.sunk | while | flops 383383040 | bytes 6944983 | solution.py:75
  12.1 0.7 add_compare_fusion.6
  12.8 2.2 fusion.74
  15.4 1.6 fusion.77
  17.1 0.7 add_compare_fusion.6
  17.8 2.2 fusion.74
  20.4 1.6 fusion.77
  22.0 28.5 %all-gather = f32[8192]{0:T(1024)S(1)} all-gather(f32[1024]{0:T(1024)S(1)} %get-tuple-element.585), channel_id=2, replica_groups=mesh['tm'=8,'particle'=8,'cell'=8] {'cell'}, dimensions={0}, use_global_device_ids=true | all-gather | bytes 36864 | tf_op jit(solution)/shard_map/all_gather | solution.py:15
  50.5 28.1 %all-gather.1 = f32[8192]{0:T(1024)S(1)} all-gather(f32[1024]{0:T(1024)S(1)} %get-tuple-element.586), channel_id=3, replica_groups=mesh['tm'=8,'particle'=8,'cell'=8] {'cell'}, dimensions={0}, use_global_device_ids=true | all-gather | bytes 36864 | tf_op jit(solution)/shard_map/all_gather | solution.py:15
  78.7 33.2 %all-gather.3 = f32[8,30,1024]{2,1,0:T(8,128)S(1)} all-gather(f32[1,30,1024]{2,1,0:T(8,128)S(1)} %bitcast.48), channel_id=4, replica_groups=mesh['tm'=8,'particle'=8,'cell'=8] {'cell'}, dimensions={0}, use_global_device_ids=true | all-gather | bytes 1105920 | tf_op jit(solution)/shard_map/all_gather | solution.py:15
  111.9 0.8 while.73
  112.8 1.1 stack.2
  113.9 12.7 %all-to-all-start = ((f32[64,30,128]{2,1,0:T(8,128)}), f32[64,30,128]{2,1,0:T(8,128)S(1)}, u32[]{:S(2)}, u32[]{:S(2)}) async-start(f32[64,30,128]{2,1,0:T(8,128)} %stack.2), calls=%async_computation | async-start | bytes 2097152 | tf_op jit(solution)/shard_map/all_to_all | solution.py:115
  126.6 166.6 %all_gather.27 = f32[30,8192]{1,0:T(8,128)S(1)} all-gather(f32[30,128]{1,0:T(8,128)S(1)} %collective-permute-done.1), channel_id=1, replica_groups=mesh['tm'=8,'particle'=8,'cell'=8] {'particle','cell'}, dimensions={1}, use_global_device_ids=true | all-gather | bytes 998400 | tf_op jit(solution)/shard_map/all_gather | solution.py:120
  293.2 20.4 %while.76 = (s32[]{:T(128)}, f32[128]{0:T(128)S(1)}, f32[128]{0:T(128)S(1)}, f32[30,128]{1,0:T(8,128)S(1)}, f32[30,8192]{1,0:T(8,128)S(1)}, /*index=5*/f32[30,12...) while((s32[]{:T(128)}, f32[128]{0:T(128)S(1)}, ...), condition=%wide.region_19.20_spmd.clone, body=%wide.region_15.19_spmd.clone.sunk | while | flops 47950212 | bytes 1042103 | solution.py:75
  297.1 0.6 fusion.86
  315.0 20.4 %while.75 = (s32[]{:T(128)}, f32[128]{0:T(128)S(1)}, f32[128]{0:T(128)S(1)}, f32[30,128]{1,0:T(8,128)S(1)}, f32[30,8192]{1,0:T(8,128)S(1)}, /*index=5*/f32[30,12...) while((s32[]{:T(128)}, f32[128]{0:T(128)S(1)}, ...), condition=%wide.region_14.15_spmd.clone, body=%wide.region_10.14_spmd.clone.sunk | while | flops 47950212 | bytes 1042103 | solution.py:75
  (314 shorter events, 42.5 us)
Async XLA Ops:
  1.4 111.4 %collective-permute-start = (f32[30,128]{1,0:T(8,128)S(1)}, f32[30,128]{1,0:T(8,128)S(1)}, u32[]{:S(2)}, u32[]{:S(2)}) collective-permute-start(f32[30,128]{1,0:T(8,128)S(1)} %bitcast.56), channel_id=1, source_target_pairs={{0,64},{64,128},{128,192},{192,256},{256,320},{320,384},{384,448},... | collective-permute-start | bytes 46088 | tf_op jit(solution)/shard_map/ppermute | solution.py:27
  3.3 123.3 %collective-permute-start.1 = (f32[30,128]{1,0:T(8,128)S(1)}, f32[30,128]{1,0:T(8,128)S(1)}, u32[]{:S(2)}, u32[]{:S(2)}) collective-permute-start(f32[30,128]{1,0:T(8,128)S(1)} %bitcast.57), channel_id=1, source_target_pairs={{64,0},{128,64},{192,128},{256,192},{320,256},{384,320},{448,384},... | collective-permute-start | bytes 46088 | tf_op jit(solution)/shard_map/ppermute | solution.py:27
  113.9 199.7 %all-to-all-start = ((f32[64,30,128]{2,1,0:T(8,128)}), f32[64,30,128]{2,1,0:T(8,128)S(1)}, u32[]{:S(2)}, u32[]{:S(2)}) async-start(f32[64,30,128]{2,1,0:T(8,128)} %stack.2), calls=%async_computation | async-start | bytes 2097152 | tf_op jit(solution)/shard_map/all_to_all | solution.py:115
  314.9 20.4 %copy-start = (f32[1,30,128]{2,0,1:T(1,128)S(1)}, f32[1,30,128]{2,0,1:T(1,128)}, u32[]{:S(2)}) copy-start(f32[1,30,128]{2,0,1:T(1,128)} %param.15) | copy-start | bytes 46084
